TPU v7x, 32 devices: a whole 2x2x4 slice. The times are simulated.
32 devices in a mesh: seg: 16 (over z, y, x), samp: 2 (over core).
Axes of the slice: x: 2, y: 2, z: 4, core: 2. Of those that a mesh axis runs over, the one named last changes fastest.
Arguments:
- rigidity_diagonal_cells: bfloat16 [512, 128, 128], P('seg')
- rigidity_lower_cells: bfloat16 [512, 128, 128], P('seg'), may hold values from -0.5 to 0.5
- inverse_diagonal_cells: bfloat16 [512, 128, 128], P('seg')
- bedding_rigidity_per_unknown: float32 [512, 128], P('seg'), may hold values from 0.3 to 2
- bedding_regime: int32 [512], P('seg'), may hold values from 0 to 2
- dilation_push_per_kelvin: float32 [512, 128], P('seg'), may hold values from 1 to 16
- heat_shape_functions: bfloat16 [512, 512], P('seg'), may hold values from -0.25 to 0.25
- sampled_shape_weights: bfloat16 [64, 512], P('samp'), may hold values from -6 to 6
- joined_segment_table: int32 [16, 2], P('seg'), may hold values from 0 to 15
- joint_rigidity: float32 [16, 2], P('seg'), may hold values from 1.2 to 3.6
Outputs:
- displacement: float32 [64, 512, 128], P('samp', 'seg')
- kl_grad: float32 [512], replicated
Inputs may be any that keep to these rules, and one draw needn't show every extreme that they name: `joined_segment_table`: every entry names a segment.
All inputs are finite; a program needn't handle non-finite values.
Results may differ from a plain program's by a relative error of at most 0.013.
Values may be sent and summed in bfloat16 or wider, within the bound.
A program may use at most 64 MiB of HBM per device.

v0:
```python
import math
import jax
import jax.numpy as jnp
from jax import lax
from jax.sharding import PartitionSpec as P

STEPS = 4


def shifted(value, axis, steps):
    count = lax.axis_size(axis)
    first, last = (max(0, -steps), min(count, count - steps))
    return lax.ppermute(value, axis, [(source, source + steps) for source in range(first, last)])


def stiffness(
    field_round, rigidity_diagonal_cells, rigidity_lower_cells, joined_segment_table, joint_rigidity
):
    own_term = jnp.einsum(
        "sjb,jab->sja", field_round, rigidity_diagonal_cells, preferred_element_type=jnp.float32
    )
    upward = jnp.einsum(
        "sjb,jba->sja", field_round, rigidity_lower_cells, preferred_element_type=jnp.float32
    ).astype(jnp.bfloat16)
    below_rim = shifted(field_round[:, -1:, :], "seg", 1)
    above_rim = shifted(upward[:, :1, :], "seg", -1)
    interfaces = lax.all_gather(field_round[:, :1, :], "seg", axis=1, tiled=True)
    lower_field = jnp.concatenate([below_rim, field_round[:, :-1]], axis=1)
    below_term = jnp.einsum(
        "sjb,jab->sja", lower_field, rigidity_lower_cells, preferred_element_type=jnp.float32
    )
    upper_term = jnp.concatenate([upward[:, 1:], above_rim], axis=1).astype(jnp.float32)
    result = own_term + below_term + upper_term
    partner = jnp.take(interfaces, joined_segment_table[0], axis=1).astype(jnp.float32)
    own_interface = field_round[:, 0:1, :].astype(jnp.float32)
    spring = jnp.sum(joint_rigidity[0][None, :, None] * (own_interface - partner), axis=1)
    return result.at[:, 0, :].add(spring)


def ballast(state, bedding_rigidity_per_unknown, bedding_regime):
    code = bedding_regime[None, :, None]
    stiff = bedding_rigidity_per_unknown[None]
    magnitude = 1.0 + jnp.abs(state)
    slide = jnp.tanh(state)
    force = jnp.where(
        code == 0, stiff * state, jnp.where(code == 1, stiff * state / magnitude, stiff * slide)
    )
    tangent = jnp.where(
        code == 0,
        stiff + 0.0 * state,
        jnp.where(code == 1, stiff / (magnitude * magnitude), stiff * (1.0 - slide * slide)),
    )
    return (force, tangent)


def blockwise(inverse_diagonal_cells, field_round):
    return jnp.einsum(
        "jab,sjb->sja", inverse_diagonal_cells, field_round, preferred_element_type=jnp.float32
    )


def body(
    rigidity_diagonal_cells,
    rigidity_lower_cells,
    inverse_diagonal_cells,
    bedding_rigidity_per_unknown,
    bedding_regime,
    dilation_push_per_kelvin,
    heat_shape_functions,
    sampled_shape_weights,
    joined_segment_table,
    joint_rigidity,
):
    samples_here = sampled_shape_weights.shape[0]
    blocks_here = rigidity_diagonal_cells.shape[0]
    width = rigidity_diagonal_cells.shape[1]
    shape_functions = heat_shape_functions.shape[1]
    complete_shape_functions = heat_shape_functions.astype(jnp.float32)
    heat_distribution = jnp.dot(
        sampled_shape_weights, heat_shape_functions.T, preferred_element_type=jnp.float32
    )
    heat_driven_source = dilation_push_per_kelvin[None] * heat_distribution[:, :, None]
    state = jnp.zeros((samples_here, blocks_here, width), jnp.float32)
    grad_total = jnp.zeros((shape_functions,), jnp.float32)
    for iteration in range(STEPS):
        state_round = state.astype(jnp.bfloat16)
        force, tangent = ballast(state, bedding_rigidity_per_unknown, bedding_regime)
        residual_vector = (
            heat_driven_source
            - stiffness(
                state_round,
                rigidity_diagonal_cells,
                rigidity_lower_cells,
                joined_segment_table,
                joint_rigidity,
            )
            - force
        )
        initial_newton_step = blockwise(
            inverse_diagonal_cells, residual_vector.astype(jnp.bfloat16)
        )
        second = (
            residual_vector
            - stiffness(
                initial_newton_step.astype(jnp.bfloat16),
                rigidity_diagonal_cells,
                rigidity_lower_cells,
                joined_segment_table,
                joint_rigidity,
            )
            - tangent * initial_newton_step
        )
        state = (
            state
            + initial_newton_step
            + blockwise(inverse_diagonal_cells, second.astype(jnp.bfloat16))
        )
        adjoint = jnp.einsum(
            "sja,jab->sjb",
            state.astype(jnp.bfloat16),
            inverse_diagonal_cells,
            preferred_element_type=jnp.float32,
        )
        weighted = jnp.sum(jnp.sum(dilation_push_per_kelvin[None] * adjoint, axis=2), axis=0)
        partial_value = jnp.dot(weighted, complete_shape_functions, precision=lax.Precision.HIGHEST)
        grad_total = grad_total + lax.psum(partial_value, ("seg", "samp"))
    every_block_list = blocks_here * lax.axis_size("seg")
    all_samples = samples_here * lax.axis_size("samp")
    scale = math.sqrt(shape_functions / (every_block_list * all_samples * width))
    return (state, grad_total * scale)


def solution(mesh):
    placed = (
        P("seg", None, None),
        P("seg", None, None),
        P("seg", None, None),
        P("seg", None),
        P("seg"),
        P("seg", None),
        P("seg", None),
        P("samp", None),
        P("seg", None),
        P("seg", None),
    )
    return jax.shard_map(
        body, mesh=mesh, in_specs=placed, out_specs=(P("samp", "seg", None), P()), check_vma=False
    )
```

profile of v0, /device:TPU:14, one launch (start us, length us, event | category | flops | bytes accessed | tf_op | source)
XLA Modules:
  0.0 460.8 jit_solution(1154479130879753834)
XLA Ops:
  0.7 3.5 collective-permute-start
  4.6 2.6 collective-permute-start.1
  17.6 4.8 %collective-permute-start.2 = (bf16[32,1,128]{2,0,1:T(8,128)(2,1)}, bf16[32,1,128]{2,0,1:T(8,128)(2,1)}, u32[]{:S(2)}, u32[]{:S(2)}) collective-permute-start(bf16[32,1,128]{2,0,1:T(8,128)(2,1)} %get-tuple-element.125), channel_id=1, source_target_pairs={{0,2},{2,4},{4,6},{6,8},{8,10},{10,12},{12,14},{14,16},{16,18},{18... | collective-permute-start | bytes 24584 | tf_op jit(solution)/shard_map/ppermute | solution.py:13
  22.4 30.9 %all_gather.22 = bf16[32,16,128]{2,0,1:T(8,128)(2,1)} all-gather(bf16[32,1,128]{2,0,1:T(8,128)(2,1)S(1)} %get-tuple-element.124), channel_id=1, replica_groups=mesh['seg'=16,'samp'=2] {'seg'}, dimensions={1}, use_global_device_ids=true | all-gather | bytes 139264 | tf_op jit(solution)/shard_map/all_gather | solution.py:27
  55.5 3.5 collective-permute-start.3
  59.1 4.1 collective-permute-done.3
  69.9 3.9 collective-permute-start.4
  73.8 34.6 %all_gather.23 = bf16[32,16,128]{2,0,1:T(8,128)(2,1)} all-gather(bf16[32,1,128]{2,0,1:T(8,128)(2,1)S(1)} %get-tuple-element.121), channel_id=1, replica_groups=mesh['seg'=16,'samp'=2] {'seg'}, dimensions={1}, use_global_device_ids=true | all-gather | bytes 139264 | tf_op jit(solution)/shard_map/all_gather | solution.py:27
  112.6 5.3 %collective-permute-done.5 = bf16[32,1,128]{2,0,1:T(8,128)(2,1)S(1)} collective-permute-done((bf16[32,1,128]{2,0,1:T(8,128)(2,1)S(1)}, bf16[32,1,128]{2,0,1:T(8,128)(2,1)S(1)}, u32[]{:S(2)}, u32[]{:S(2)}) %collective-permute-start.5) | collective-permute-done | bytes 8224 | tf_op jit(solution)/shard_map/ppermute | solution.py:13
  124.6 1.9 collective-permute-start.6
  126.5 40.1 %all_gather.24 = bf16[32,16,128]{2,0,1:T(8,128)(2,1)} all-gather(bf16[32,1,128]{2,0,1:T(8,128)(2,1)S(1)} %get-tuple-element.118), channel_id=1, replica_groups=mesh['seg'=16,'samp'=2] {'seg'}, dimensions={1}, use_global_device_ids=true | all-gather | bytes 139264 | tf_op jit(solution)/shard_map/all_gather | solution.py:27
  170.9 5.2 %collective-permute-done.7 = bf16[32,1,128]{2,0,1:T(8,128)(2,1)S(1)} collective-permute-done((bf16[32,1,128]{2,0,1:T(8,128)(2,1)S(1)}, bf16[32,1,128]{2,0,1:T(8,128)(2,1)S(1)}, u32[]{:S(2)}, u32[]{:S(2)}) %collective-permute-start.7) | collective-permute-done | bytes 8224 | tf_op jit(solution)/shard_map/ppermute | solution.py:13
  186.0 40.2 %all_gather.25 = bf16[32,16,128]{2,0,1:T(8,128)(2,1)} all-gather(bf16[32,1,128]{2,0,1:T(8,128)(2,1)S(1)} %get-tuple-element.115), channel_id=1, replica_groups=mesh['seg'=16,'samp'=2] {'seg'}, dimensions={1}, use_global_device_ids=true | all-gather | bytes 139264 | tf_op jit(solution)/shard_map/all_gather | solution.py:27
  230.5 5.3 %collective-permute-done.9 = bf16[32,1,128]{2,0,1:T(8,128)(2,1)S(1)} collective-permute-done((bf16[32,1,128]{2,0,1:T(8,128)(2,1)S(1)}, bf16[32,1,128]{2,0,1:T(8,128)(2,1)S(1)}, u32[]{:S(2)}, u32[]{:S(2)}) %collective-permute-start.9) | collective-permute-done | bytes 8224 | tf_op jit(solution)/shard_map/ppermute | solution.py:13
  244.4 40.1 %all_gather.26 = bf16[32,16,128]{2,0,1:T(8,128)(2,1)} all-gather(bf16[32,1,128]{2,0,1:T(8,128)(2,1)S(1)} %get-tuple-element.112), channel_id=1, replica_groups=mesh['seg'=16,'samp'=2] {'seg'}, dimensions={1}, use_global_device_ids=true | all-gather | bytes 139264 | tf_op jit(solution)/shard_map/all_gather | solution.py:27
  286.6 2.1 collective-permute-start.11
  288.9 5.0 %collective-permute-done.11 = bf16[32,1,128]{2,0,1:T(8,128)(2,1)S(1)} collective-permute-done((bf16[32,1,128]{2,0,1:T(8,128)(2,1)S(1)}, bf16[32,1,128]{2,0,1:T(8,128)(2,1)S(1)}, u32[]{:S(2)}, u32[]{:S(2)}) %collective-permute-start.11) | collective-permute-done | bytes 8224 | tf_op jit(solution)/shard_map/ppermute | solution.py:13
  303.9 40.1 %all_gather.27 = bf16[32,16,128]{2,0,1:T(8,128)(2,1)} all-gather(bf16[32,1,128]{2,0,1:T(8,128)(2,1)S(1)} %get-tuple-element.109), channel_id=1, replica_groups=mesh['seg'=16,'samp'=2] {'seg'}, dimensions={1}, use_global_device_ids=true | all-gather | bytes 139264 | tf_op jit(solution)/shard_map/all_gather | solution.py:27
  346.1 2.0 collective-permute-start.13
  348.2 5.2 %collective-permute-done.13 = bf16[32,1,128]{2,0,1:T(8,128)(2,1)S(1)} collective-permute-done((bf16[32,1,128]{2,0,1:T(8,128)(2,1)S(1)}, bf16[32,1,128]{2,0,1:T(8,128)(2,1)S(1)}, u32[]{:S(2)}, u32[]{:S(2)}) %collective-permute-start.13) | collective-permute-done | bytes 8224 | tf_op jit(solution)/shard_map/ppermute | solution.py:13
  361.5 37.3 %all_gather.28 = bf16[32,16,128]{2,0,1:T(8,128)(2,1)S(1)} all-gather(bf16[32,1,128]{2,0,1:T(8,128)(2,1)S(1)} %get-tuple-element.106), channel_id=1, replica_groups=mesh['seg'=16,'samp'=2] {'seg'}, dimensions={1}, use_global_device_ids=true | all-gather | bytes 139264 | tf_op jit(solution)/shard_map/all_gather | solution.py:27
  400.1 2.0 collective-permute-start.15
  402.2 5.2 %collective-permute-done.15 = bf16[32,1,128]{2,0,1:T(8,128)(2,1)S(1)} collective-permute-done((bf16[32,1,128]{2,0,1:T(8,128)(2,1)S(1)}, bf16[32,1,128]{2,0,1:T(8,128)(2,1)S(1)}, u32[]{:S(2)}, u32[]{:S(2)}) %collective-permute-start.15) | collective-permute-done | bytes 8224 | tf_op jit(solution)/shard_map/ppermute | solution.py:13
  412.1 48.0 %psum.34 = f32[512]{0:T(512)S(1)} all-reduce(f32[512]{0:T(512)S(1)} %add_add_fusion), channel_id=1, replica_groups=mesh['seg'=16,'samp'=2] {'seg','samp'}, use_global_device_ids=true, to_apply=%region_9.11 | all-reduce | flops 512 | bytes 4096 | tf_op jit(solution)/shard_map/psum | solution.py:126
  (234 shorter events, 86.2 us)
Async XLA Ops:
  0.6 7.8 %copy-start.1 = (bf16[32,128,128]{2,1,0:T(8,128)(2,1)S(1)}, bf16[32,128,128]{2,1,0:T(8,128)(2,1)}, u32[]{:S(2)}) copy-start(bf16[32,128,128]{2,1,0:T(8,128)(2,1)} %param.28) | copy-start | bytes 3145732
  0.7 10.2 %collective-permute-start = (bf16[32,1,128]{2,0,1:T(8,128)(2,1)S(1)}, bf16[32,1,128]{2,0,1:T(8,128)(2,1)S(1)}, u32[]{:S(2)}, u32[]{:S(2)}) collective-permute-start(bf16[32,1,128]{2,0,1:T(8,128)(2,1)S(1)} %slice.302), channel_id=1, source_target_pairs={{0,2},{2,4},{4,6},{6,8},{8,10},{10,12},{12,14},{14,16},{16,18},{18... | collective-permute-start | bytes 24584 | tf_op jit(solution)/shard_map/ppermute | solution.py:13
  4.6 7.5 %collective-permute-start.1 = (bf16[32,1,128]{2,0,1:T(8,128)(2,1)S(1)}, bf16[32,1,128]{2,0,1:T(8,128)(2,1)S(1)}, u32[]{:S(2)}, u32[]{:S(2)}) collective-permute-start(bf16[32,1,128]{2,0,1:T(8,128)(2,1)S(1)} %slice.366), channel_id=1, source_target_pairs={{2,0},{4,2},{6,4},{8,6},{10,8},{12,10},{14,12},{16,14},{18,16},{20... | collective-permute-start | bytes 24584 | tf_op jit(solution)/shard_map/ppermute | solution.py:13
  14.3 44.7 %copy-start.7 = (bf16[32,32,128]{2,0,1:T(8,128)(2,1)}, bf16[32,32,128]{2,0,1:T(8,128)(2,1)S(1)}, u32[]{:S(2)}) copy-start(bf16[32,32,128]{2,0,1:T(8,128)(2,1)S(1)} %convert_bitcast_fusion) | copy-start | bytes 786436
  17.6 41.5 %collective-permute-start.2 = (bf16[32,1,128]{2,0,1:T(8,128)(2,1)}, bf16[32,1,128]{2,0,1:T(8,128)(2,1)}, u32[]{:S(2)}, u32[]{:S(2)}) collective-permute-start(bf16[32,1,128]{2,0,1:T(8,128)(2,1)} %get-tuple-element.125), channel_id=1, source_target_pairs={{0,2},{2,4},{4,6},{6,8},{8,10},{10,12},{12,14},{14,16},{16,18},{18... | collective-permute-start | bytes 24584 | tf_op jit(solution)/shard_map/ppermute | solution.py:13
  55.5 7.7 %collective-permute-start.3 = (bf16[32,1,128]{2,0,1:T(8,128)(2,1)S(1)}, bf16[32,1,128]{2,0,1:T(8,128)(2,1)S(1)}, u32[]{:S(2)}, u32[]{:S(2)}) collective-permute-start(bf16[32,1,128]{2,0,1:T(8,128)(2,1)S(1)} %slice.371), channel_id=1, source_target_pairs={{2,0},{4,2},{6,4},{8,6},{10,8},{12,10},{14,12},{16,14},{18,16},{20... | collective-permute-start | bytes 24584 | tf_op jit(solution)/shard_map/ppermute | solution.py:13
  69.9 42.7 %collective-permute-start.4 = (bf16[32,1,128]{2,0,1:T(8,128)(2,1)}, bf16[32,1,128]{2,0,1:T(8,128)(2,1)}, u32[]{:S(2)}, u32[]{:S(2)}) collective-permute-start(bf16[32,1,128]{2,0,1:T(8,128)(2,1)} %get-tuple-element.122), channel_id=1, source_target_pairs={{0,2},{2,4},{4,6},{6,8},{8,10},{10,12},{12,14},{14,16},{16,18},{18... | collective-permute-start | bytes 24584 | tf_op jit(solution)/shard_map/ppermute | solution.py:13
  110.5 7.3 %collective-permute-start.5 = (bf16[32,1,128]{2,0,1:T(8,128)(2,1)S(1)}, bf16[32,1,128]{2,0,1:T(8,128)(2,1)S(1)}, u32[]{:S(2)}, u32[]{:S(2)}) collective-permute-start(bf16[32,1,128]{2,0,1:T(8,128)(2,1)S(1)} %slice.377), channel_id=1, source_target_pairs={{2,0},{4,2},{6,4},{8,6},{10,8},{12,10},{14,12},{16,14},{18,16},{20... | collective-permute-start | bytes 24584 | tf_op jit(solution)/shard_map/ppermute | solution.py:13
  112.6 6.7 %copy-start.24 = (f32[32,32,128]{2,0,1:T(8,128)S(1)}, f32[32,32,128]{2,0,1:T(8,128)}, u32[]{:S(2)}) copy-start(f32[32,32,128]{2,0,1:T(8,128)} %get-tuple-element.129) | copy-start | bytes 1572868
  124.6 46.3 %collective-permute-start.6 = (bf16[32,1,128]{2,0,1:T(8,128)(2,1)}, bf16[32,1,128]{2,0,1:T(8,128)(2,1)}, u32[]{:S(2)}, u32[]{:S(2)}) collective-permute-start(bf16[32,1,128]{2,0,1:T(8,128)(2,1)} %get-tuple-element.119), channel_id=1, source_target_pairs={{0,2},{2,4},{4,6},{6,8},{8,10},{10,12},{12,14},{14,16},{16,18},{18... | collective-permute-start | bytes 24584 | tf_op jit(solution)/shard_map/ppermute | solution.py:13
  168.8 7.3 %collective-permute-start.7 = (bf16[32,1,128]{2,0,1:T(8,128)(2,1)S(1)}, bf16[32,1,128]{2,0,1:T(8,128)(2,1)S(1)}, u32[]{:S(2)}, u32[]{:S(2)}) collective-permute-start(bf16[32,1,128]{2,0,1:T(8,128)(2,1)S(1)} %slice.383), channel_id=1, source_target_pairs={{2,0},{4,2},{6,4},{8,6},{10,8},{12,10},{14,12},{16,14},{18,16},{20... | collective-permute-start | bytes 24584 | tf_op jit(solution)/shard_map/ppermute | solution.py:13
  170.8 6.7 %copy-start.19 = (f32[32,32,128]{2,0,1:T(8,128)S(1)}, f32[32,32,128]{2,0,1:T(8,128)}, u32[]{:S(2)}) copy-start(f32[32,32,128]{2,0,1:T(8,128)} %copy-done.18) | copy-start | bytes 1572868
  170.9 6.7 %copy-start.25 = (f32[32,32,128]{2,0,1:T(8,128)S(1)}, f32[32,32,128]{2,0,1:T(8,128)}, u32[]{:S(2)}) copy-start(f32[32,32,128]{2,0,1:T(8,128)} %get-tuple-element.129) | copy-start | bytes 1572868
  170.9 6.7 %copy-start.50 = (f32[32,32,128]{2,0,1:T(8,128)S(1)}, f32[32,32,128]{2,0,1:T(8,128)}, u32[]{:S(2)}) copy-start(f32[32,32,128]{2,0,1:T(8,128)} %get-tuple-element.131) | copy-start | bytes 1572868
  184.1 46.4 %collective-permute-start.8 = (bf16[32,1,128]{2,0,1:T(8,128)(2,1)}, bf16[32,1,128]{2,0,1:T(8,128)(2,1)}, u32[]{:S(2)}, u32[]{:S(2)}) collective-permute-start(bf16[32,1,128]{2,0,1:T(8,128)(2,1)} %get-tuple-element.116), channel_id=1, source_target_pairs={{0,2},{2,4},{4,6},{6,8},{8,10},{10,12},{12,14},{14,16},{16,18},{18... | collective-permute-start | bytes 24584 | tf_op jit(solution)/shard_map/ppermute | solution.py:13
  228.4 7.3 %collective-permute-start.9 = (bf16[32,1,128]{2,0,1:T(8,128)(2,1)S(1)}, bf16[32,1,128]{2,0,1:T(8,128)(2,1)S(1)}, u32[]{:S(2)}, u32[]{:S(2)}) collective-permute-start(bf16[32,1,128]{2,0,1:T(8,128)(2,1)S(1)} %slice.389), channel_id=1, source_target_pairs={{2,0},{4,2},{6,4},{8,6},{10,8},{12,10},{14,12},{16,14},{18,16},{20... | collective-permute-start | bytes 24584 | tf_op jit(solution)/shard_map/ppermute | solution.py:13
  230.5 6.7 %copy-start.47 = (f32[32,32,128]{2,0,1:T(8,128)S(1)}, f32[32,32,128]{2,0,1:T(8,128)}, u32[]{:S(2)}) copy-start(f32[32,32,128]{2,0,1:T(8,128)} %get-tuple-element.133) | copy-start | bytes 1572868
  242.5 46.4 %collective-permute-start.10 = (bf16[32,1,128]{2,0,1:T(8,128)(2,1)}, bf16[32,1,128]{2,0,1:T(8,128)(2,1)}, u32[]{:S(2)}, u32[]{:S(2)}) collective-permute-start(bf16[32,1,128]{2,0,1:T(8,128)(2,1)} %get-tuple-element.113), channel_id=1, source_target_pairs={{0,2},{2,4},{4,6},{6,8},{8,10},{10,12},{12,14},{14,16},{16,18},{18... | collective-permute-start | bytes 24584 | tf_op jit(solution)/shard_map/ppermute | solution.py:13
  286.6 7.3 %collective-permute-start.11 = (bf16[32,1,128]{2,0,1:T(8,128)(2,1)S(1)}, bf16[32,1,128]{2,0,1:T(8,128)(2,1)S(1)}, u32[]{:S(2)}, u32[]{:S(2)}) collective-permute-start(bf16[32,1,128]{2,0,1:T(8,128)(2,1)S(1)} %slice.395), channel_id=1, source_target_pairs={{2,0},{4,2},{6,4},{8,6},{10,8},{12,10},{14,12},{16,14},{18,16},{20... | collective-permute-start | bytes 24584 | tf_op jit(solution)/shard_map/ppermute | solution.py:13
  301.9 46.3 %collective-permute-start.12 = (bf16[32,1,128]{2,0,1:T(8,128)(2,1)}, bf16[32,1,128]{2,0,1:T(8,128)(2,1)}, u32[]{:S(2)}, u32[]{:S(2)}) collective-permute-start(bf16[32,1,128]{2,0,1:T(8,128)(2,1)} %get-tuple-element.110), channel_id=1, source_target_pairs={{0,2},{2,4},{4,6},{6,8},{8,10},{10,12},{12,14},{14,16},{16,18},{18... | collective-permute-start | bytes 24584 | tf_op jit(solution)/shard_map/ppermute | solution.py:13
  346.1 7.3 %collective-permute-start.13 = (bf16[32,1,128]{2,0,1:T(8,128)(2,1)S(1)}, bf16[32,1,128]{2,0,1:T(8,128)(2,1)S(1)}, u32[]{:S(2)}, u32[]{:S(2)}) collective-permute-start(bf16[32,1,128]{2,0,1:T(8,128)(2,1)S(1)} %slice.401), channel_id=1, source_target_pairs={{2,0},{4,2},{6,4},{8,6},{10,8},{12,10},{14,12},{16,14},{18,16},{20... | collective-permute-start | bytes 24584 | tf_op jit(solution)/shard_map/ppermute | solution.py:13
  348.2 6.7 %copy-start.45 = (f32[32,32,128]{2,0,1:T(8,128)S(1)}, f32[32,32,128]{2,0,1:T(8,128)}, u32[]{:S(2)}) copy-start(f32[32,32,128]{2,0,1:T(8,128)} %get-tuple-element.137) | copy-start | bytes 1572868
  359.6 42.6 %collective-permute-start.14 = (bf16[32,1,128]{2,0,1:T(8,128)(2,1)S(1)}, bf16[32,1,128]{2,0,1:T(8,128)(2,1)S(1)}, u32[]{:S(2)}, u32[]{:S(2)}) collective-permute-start(bf16[32,1,128]{2,0,1:T(8,128)(2,1)S(1)} %get-tuple-element.107), channel_id=1, source_target_pairs={{0,2},{2,4},{4,6},{6,8},{8,10},{10,12},{12,14},{14,16},{16,18},{18... | collective-permute-start | bytes 24584 | tf_op jit(solution)/shard_map/ppermute | solution.py:13
  400.1 7.3 %collective-permute-start.15 = (bf16[32,1,128]{2,0,1:T(8,128)(2,1)S(1)}, bf16[32,1,128]{2,0,1:T(8,128)(2,1)S(1)}, u32[]{:S(2)}, u32[]{:S(2)}) collective-permute-start(bf16[32,1,128]{2,0,1:T(8,128)(2,1)S(1)} %slice.407), channel_id=1, source_target_pairs={{2,0},{4,2},{6,4},{8,6},{10,8},{12,10},{14,12},{16,14},{18,16},{20... | collective-permute-start | bytes 24584 | tf_op jit(solution)/shard_map/ppermute | solution.py:13
  (52 other events, 161.3 us)
where the time goes:
time: 462 us; the launch traced here: 461 us
  blocking collectives  311 us (67%)
  matrix products  43.6 us (9%)
  starting transfers between devices  39.7 us (9%)
  waiting for transfers between devices  36.5 us (8%)
  local copies, waits for them, and re-layouts  22.3 us (5%)
  other arithmetic  5.63 us (1%)
    all_gather x7, blocking collectives, stiffness(): lax.all_gather(field_round[:, :1, :], 'seg', axis=1, tiled=True)  263 us
    psum x1, blocking collectives, body(): grad_total = grad_total + lax.psum(partial_value, ('seg', 'samp'))  48 us
    ppermute x16, starting transfers between devices, shifted(): lax.ppermute(value, axis, [(source, source + steps) for source in range(f...  39.7 us
    ppermute x16, waiting for transfers between devices, shifted(): lax.ppermute(value, axis, [(source, source + steps) for source in range(f...  36.5 us
    dot_general x8, matrix products, stiffness(): jnp.einsum('sjb,jab->sja', field_round, rigidity_diagonal_cells, preferre...  11.7 us
    dot_general x8, matrix products, blockwise(): jnp.einsum('jab,sjb->sja', inverse_diagonal_cells, field_round, preferred...  10.8 us
    gather x8, local copies, waits for them, and re-layouts, stiffness(): jnp.take(interfaces, joined_segment_table[0], axis=1).astype(jnp.float32)  9.89 us
    dot_general x8, matrix products, stiffness(): jnp.einsum('sjb,jab->sja', lower_field, rigidity_lower_cells, preferred_e...  9.37 us
  transfers between devices with their start and end apart: 16, of which 8 were waited for; matrix products, arithmetic and copies ran while one was open for 4% of the time, Pallas kernels for 0%

commit v1 on v0

--- a/solution.py
+++ b/solution.py
@@ -123,7 +123,7 @@
         )
         weighted = jnp.sum(jnp.sum(dilation_push_per_kelvin[None] * adjoint, axis=2), axis=0)
         partial_value = jnp.dot(weighted, complete_shape_functions, precision=lax.Precision.HIGHEST)
-        grad_total = grad_total + lax.psum(partial_value, ("seg", "samp"))
+        grad_total = grad_total + jnp.sum(lax.all_gather(partial_value, ("seg", "samp")), axis=0)
     every_block_list = blocks_here * lax.axis_size("seg")
     all_samples = samples_here * lax.axis_size("samp")
     scale = math.sqrt(shape_functions / (every_block_list * all_samples * width))

time: 462 us -> 568 us (1.23)
  the two profiles are of different devices: /device:TPU:14 before, /device:TPU:0 now
where the time goes in v1:
time: 568 us; the launch traced here: 566 us
  blocking collectives  427 us (75%)
  matrix products  44.3 us (8%)
  starting transfers between devices  38.6 us (7%)
  local copies, waits for them, and re-layouts  28.2 us (5%)
  waiting for transfers between devices  16.6 us (3%)
  other arithmetic  10 us (2%)
    all_gather x7, blocking collectives, stiffness(): lax.all_gather(field_round[:, :1, :], 'seg', axis=1, tiled=True)  270 us
    all_gather x4, blocking collectives, body(): lax.all_gather(partial_value, ('seg', 'samp'))  157 us
    ppermute x16, starting transfers between devices, shifted(): lax.ppermute(value, axis, [(source, source + steps) for source in range(f...  38.6 us
    ppermute x16, waiting for transfers between devices, shifted(): lax.ppermute(value, axis, [(source, source + steps) for source in range(f...  16.6 us
    dot_general x8, matrix products, stiffness(): jnp.einsum('sjb,jab->sja', field_round, rigidity_diagonal_cells, preferre...  11.6 us
  transfers between devices with their start and end apart: 16, of which 5 were waited for; matrix products, arithmetic and copies ran while one was open for 5% of the time, Pallas kernels for 0%

profile of v1, /device:TPU:0, one launch (start us, length us, event | category | flops | bytes accessed | tf_op | source)
XLA Modules:
  0.0 566.3 jit_solution(1376135916882519714)
XLA Ops:
  0.7 5.0 collective-permute-start
  17.6 5.1 collective-permute-start.2
  22.7 41.3 %all_gather.46 = bf16[32,16,128]{2,0,1:T(8,128)(2,1)} all-gather(bf16[32,1,128]{2,0,1:T(8,128)(2,1)S(1)} %get-tuple-element.124), channel_id=1, replica_groups=mesh['seg'=16,'samp'=2] {'seg'}, dimensions={1}, use_global_device_ids=true | all-gather | bytes 139264 | tf_op jit(solution)/shard_map/all_gather | solution.py:27
  67.8 4.1 collective-permute-done.3
  79.2 2.6 collective-permute-start.4
  81.8 38.5 %all_gather.47 = bf16[32,16,128]{2,0,1:T(8,128)(2,1)} all-gather(bf16[32,1,128]{2,0,1:T(8,128)(2,1)S(1)} %get-tuple-element.121), channel_id=1, replica_groups=mesh['seg'=16,'samp'=2] {'seg'}, dimensions={1}, use_global_device_ids=true | all-gather | bytes 139264 | tf_op jit(solution)/shard_map/all_gather | solution.py:27
  125.2 39.3 %all-gather.4 = f32[32,1,512]{2,1,0:T(1,128)S(1)} all-gather(f32[1,1,512]{2,1,0:T(1,128)S(1)} %copy-done.44), channel_id=2, replica_groups=mesh['seg'=16,'samp'=2] {'seg','samp'}, dimensions={0}, use_global_device_ids=true | all-gather | bytes 67584 | tf_op jit(solution)/shard_map/all_gather | solution.py:126
  166.2 1.8 fusion.9
  174.7 38.5 %all_gather.48 = bf16[32,16,128]{2,0,1:T(8,128)(2,1)} all-gather(bf16[32,1,128]{2,0,1:T(8,128)(2,1)S(1)} %get-tuple-element.118), channel_id=1, replica_groups=mesh['seg'=16,'samp'=2] {'seg'}, dimensions={1}, use_global_device_ids=true | all-gather | bytes 139264 | tf_op jit(solution)/shard_map/all_gather | solution.py:27
  217.0 4.1 collective-permute-done.7
  228.4 5.4 collective-permute-start.8
  233.8 38.5 %all_gather.49 = bf16[32,16,128]{2,0,1:T(8,128)(2,1)} all-gather(bf16[32,1,128]{2,0,1:T(8,128)(2,1)S(1)} %get-tuple-element.115), channel_id=1, replica_groups=mesh['seg'=16,'samp'=2] {'seg'}, dimensions={1}, use_global_device_ids=true | all-gather | bytes 139264 | tf_op jit(solution)/shard_map/all_gather | solution.py:27
  277.1 39.3 %all-gather.5 = f32[32,1,512]{2,1,0:T(1,128)S(1)} all-gather(f32[1,1,512]{2,1,0:T(1,128)S(1)} %copy-done.45), channel_id=3, replica_groups=mesh['seg'=16,'samp'=2] {'seg','samp'}, dimensions={0}, use_global_device_ids=true | all-gather | bytes 67584 | tf_op jit(solution)/shard_map/all_gather | solution.py:126
  318.0 1.8 fusion.11
  326.5 38.5 %all_gather.50 = bf16[32,16,128]{2,0,1:T(8,128)(2,1)} all-gather(bf16[32,1,128]{2,0,1:T(8,128)(2,1)S(1)} %get-tuple-element.112), channel_id=1, replica_groups=mesh['seg'=16,'samp'=2] {'seg'}, dimensions={1}, use_global_device_ids=true | all-gather | bytes 139264 | tf_op jit(solution)/shard_map/all_gather | solution.py:27
  367.3 1.6 collective-permute-start.11
  369.1 3.9 collective-permute-done.11
  380.2 5.4 collective-permute-start.12
  385.6 38.5 %all_gather.51 = bf16[32,16,128]{2,0,1:T(8,128)(2,1)} all-gather(bf16[32,1,128]{2,0,1:T(8,128)(2,1)S(1)} %get-tuple-element.109), channel_id=1, replica_groups=mesh['seg'=16,'samp'=2] {'seg'}, dimensions={1}, use_global_device_ids=true | all-gather | bytes 139264 | tf_op jit(solution)/shard_map/all_gather | solution.py:27
  428.9 39.3 %all-gather.6 = f32[32,1,512]{2,1,0:T(1,128)S(1)} all-gather(f32[1,1,512]{2,1,0:T(1,128)S(1)} %copy-done.46), channel_id=4, replica_groups=mesh['seg'=16,'samp'=2] {'seg','samp'}, dimensions={0}, use_global_device_ids=true | all-gather | bytes 67584 | tf_op jit(solution)/shard_map/all_gather | solution.py:126
  469.9 1.8 fusion.13
  478.4 36.1 %all_gather.52 = bf16[32,16,128]{2,0,1:T(8,128)(2,1)S(1)} all-gather(bf16[32,1,128]{2,0,1:T(8,128)(2,1)S(1)} %get-tuple-element.106), channel_id=1, replica_groups=mesh['seg'=16,'samp'=2] {'seg'}, dimensions={1}, use_global_device_ids=true | all-gather | bytes 139264 | tf_op jit(solution)/shard_map/all_gather | solution.py:27
  517.5 4.1 collective-permute-done.15
  525.6 39.4 %all-gather.7 = f32[32,1,512]{2,1,0:T(1,128)S(1)} all-gather(f32[1,1,512]{2,1,0:T(1,128)S(1)} %convolution_bitcast_fusion.6), channel_id=5, replica_groups=mesh['seg'=16,'samp'=2] {'seg','samp'}, dimensions={0}, use_global_device_ids=true | all-gather | bytes 67584 | tf_op jit(solution)/shard_map/all_gather | solution.py:126
  (272 shorter events, 91.0 us)
Async XLA Ops:
  0.6 5.0 copy-start
  0.6 8.2 %copy-start.1 = (bf16[32,128,128]{2,1,0:T(8,128)(2,1)S(1)}, bf16[32,128,128]{2,1,0:T(8,128)(2,1)}, u32[]{:S(2)}) copy-start(bf16[32,128,128]{2,1,0:T(8,128)(2,1)} %param.28) | copy-start | bytes 3145732
  0.7 10.6 %collective-permute-start = (bf16[32,1,128]{2,0,1:T(8,128)(2,1)S(1)}, bf16[32,1,128]{2,0,1:T(8,128)(2,1)S(1)}, u32[]{:S(2)}, u32[]{:S(2)}) collective-permute-start(bf16[32,1,128]{2,0,1:T(8,128)(2,1)S(1)} %slice.302), channel_id=1, source_target_pairs={{0,2},{2,4},{4,6},{6,8},{8,10},{10,12},{12,14},{14,16},{16,18},{18... | collective-permute-start | bytes 24584 | tf_op jit(solution)/shard_map/ppermute | solution.py:13
  6.1 5.7 %collective-permute-start.1 = (bf16[32,1,128]{2,0,1:T(8,128)(2,1)S(1)}, bf16[32,1,128]{2,0,1:T(8,128)(2,1)S(1)}, u32[]{:S(2)}, u32[]{:S(2)}) collective-permute-start(bf16[32,1,128]{2,0,1:T(8,128)(2,1)S(1)} %slice.366), channel_id=1, source_target_pairs={{2,0},{4,2},{6,4},{8,6},{10,8},{12,10},{14,12},{16,14},{18,16},{20... | collective-permute-start | bytes 24584 | tf_op jit(solution)/shard_map/ppermute | solution.py:13
  14.3 53.4 %copy-start.7 = (bf16[32,32,128]{2,0,1:T(8,128)(2,1)}, bf16[32,32,128]{2,0,1:T(8,128)(2,1)S(1)}, u32[]{:S(2)}) copy-start(bf16[32,32,128]{2,0,1:T(8,128)(2,1)S(1)} %convert_bitcast_fusion) | copy-start | bytes 786436
  17.6 50.2 %collective-permute-start.2 = (bf16[32,1,128]{2,0,1:T(8,128)(2,1)}, bf16[32,1,128]{2,0,1:T(8,128)(2,1)}, u32[]{:S(2)}, u32[]{:S(2)}) collective-permute-start(bf16[32,1,128]{2,0,1:T(8,128)(2,1)} %get-tuple-element.125), channel_id=1, source_target_pairs={{0,2},{2,4},{4,6},{6,8},{8,10},{10,12},{12,14},{14,16},{16,18},{18... | collective-permute-start | bytes 24584 | tf_op jit(solution)/shard_map/ppermute | solution.py:13
  66.2 5.7 %collective-permute-start.3 = (bf16[32,1,128]{2,0,1:T(8,128)(2,1)S(1)}, bf16[32,1,128]{2,0,1:T(8,128)(2,1)S(1)}, u32[]{:S(2)}, u32[]{:S(2)}) collective-permute-start(bf16[32,1,128]{2,0,1:T(8,128)(2,1)S(1)} %slice.371), channel_id=1, source_target_pairs={{2,0},{4,2},{6,4},{8,6},{10,8},{12,10},{14,12},{16,14},{18,16},{20... | collective-permute-start | bytes 24584 | tf_op jit(solution)/shard_map/ppermute | solution.py:13
  67.8 5.5 copy-start.4
  67.8 5.5 copy-start.6
  79.2 86.7 %collective-permute-start.4 = (bf16[32,1,128]{2,0,1:T(8,128)(2,1)}, bf16[32,1,128]{2,0,1:T(8,128)(2,1)}, u32[]{:S(2)}, u32[]{:S(2)}) collective-permute-start(bf16[32,1,128]{2,0,1:T(8,128)(2,1)} %get-tuple-element.122), channel_id=1, source_target_pairs={{0,2},{2,4},{4,6},{6,8},{8,10},{10,12},{12,14},{14,16},{16,18},{18... | collective-permute-start | bytes 24584 | tf_op jit(solution)/shard_map/ppermute | solution.py:13
  123.1 42.8 %collective-permute-start.5 = (bf16[32,1,128]{2,0,1:T(8,128)(2,1)}, bf16[32,1,128]{2,0,1:T(8,128)(2,1)}, u32[]{:S(2)}, u32[]{:S(2)}) collective-permute-start(bf16[32,1,128]{2,0,1:T(8,128)(2,1)} %slice.377), channel_id=1, source_target_pairs={{2,0},{4,2},{6,4},{8,6},{10,8},{12,10},{14,12},{16,14},{18,16},{20... | collective-permute-start | bytes 24584 | tf_op jit(solution)/shard_map/ppermute | solution.py:13
  173.4 43.6 %collective-permute-start.6 = (bf16[32,1,128]{2,0,1:T(8,128)(2,1)}, bf16[32,1,128]{2,0,1:T(8,128)(2,1)S(1)}, u32[]{:S(2)}, u32[]{:S(2)}) collective-permute-start(bf16[32,1,128]{2,0,1:T(8,128)(2,1)} %get-tuple-element.119), channel_id=1, source_target_pairs={{0,2},{2,4},{4,6},{6,8},{8,10},{10,12},{12,14},{14,16},{16,18},{18... | collective-permute-start | bytes 24584 | tf_op jit(solution)/shard_map/ppermute | solution.py:13
  215.4 5.7 %collective-permute-start.7 = (bf16[32,1,128]{2,0,1:T(8,128)(2,1)S(1)}, bf16[32,1,128]{2,0,1:T(8,128)(2,1)S(1)}, u32[]{:S(2)}, u32[]{:S(2)}) collective-permute-start(bf16[32,1,128]{2,0,1:T(8,128)(2,1)S(1)} %slice.383), channel_id=1, source_target_pairs={{2,0},{4,2},{6,4},{8,6},{10,8},{12,10},{14,12},{16,14},{18,16},{20... | collective-permute-start | bytes 24584 | tf_op jit(solution)/shard_map/ppermute | solution.py:13
  217.0 4.8 copy-start.16
  228.4 89.4 %collective-permute-start.8 = (bf16[32,1,128]{2,0,1:T(8,128)(2,1)}, bf16[32,1,128]{2,0,1:T(8,128)(2,1)}, u32[]{:S(2)}, u32[]{:S(2)}) collective-permute-start(bf16[32,1,128]{2,0,1:T(8,128)(2,1)} %get-tuple-element.116), channel_id=1, source_target_pairs={{0,2},{2,4},{4,6},{6,8},{8,10},{10,12},{12,14},{14,16},{16,18},{18... | collective-permute-start | bytes 24584 | tf_op jit(solution)/shard_map/ppermute | solution.py:13
  275.1 42.7 %collective-permute-start.9 = (bf16[32,1,128]{2,0,1:T(8,128)(2,1)}, bf16[32,1,128]{2,0,1:T(8,128)(2,1)}, u32[]{:S(2)}, u32[]{:S(2)}) collective-permute-start(bf16[32,1,128]{2,0,1:T(8,128)(2,1)} %slice.389), channel_id=1, source_target_pairs={{2,0},{4,2},{6,4},{8,6},{10,8},{12,10},{14,12},{16,14},{18,16},{20... | collective-permute-start | bytes 24584 | tf_op jit(solution)/shard_map/ppermute | solution.py:13
  325.3 43.8 %collective-permute-start.10 = (bf16[32,1,128]{2,0,1:T(8,128)(2,1)}, bf16[32,1,128]{2,0,1:T(8,128)(2,1)S(1)}, u32[]{:S(2)}, u32[]{:S(2)}) collective-permute-start(bf16[32,1,128]{2,0,1:T(8,128)(2,1)} %get-tuple-element.113), channel_id=1, source_target_pairs={{0,2},{2,4},{4,6},{6,8},{8,10},{10,12},{12,14},{14,16},{16,18},{18... | collective-permute-start | bytes 24584 | tf_op jit(solution)/shard_map/ppermute | solution.py:13
  367.3 5.7 %collective-permute-start.11 = (bf16[32,1,128]{2,0,1:T(8,128)(2,1)S(1)}, bf16[32,1,128]{2,0,1:T(8,128)(2,1)S(1)}, u32[]{:S(2)}, u32[]{:S(2)}) collective-permute-start(bf16[32,1,128]{2,0,1:T(8,128)(2,1)S(1)} %slice.395), channel_id=1, source_target_pairs={{2,0},{4,2},{6,4},{8,6},{10,8},{12,10},{14,12},{16,14},{18,16},{20... | collective-permute-start | bytes 24584 | tf_op jit(solution)/shard_map/ppermute | solution.py:13
  380.2 89.4 %collective-permute-start.12 = (bf16[32,1,128]{2,0,1:T(8,128)(2,1)}, bf16[32,1,128]{2,0,1:T(8,128)(2,1)}, u32[]{:S(2)}, u32[]{:S(2)}) collective-permute-start(bf16[32,1,128]{2,0,1:T(8,128)(2,1)} %get-tuple-element.110), channel_id=1, source_target_pairs={{0,2},{2,4},{4,6},{6,8},{8,10},{10,12},{12,14},{14,16},{16,18},{18... | collective-permute-start | bytes 24584 | tf_op jit(solution)/shard_map/ppermute | solution.py:13
  426.9 42.7 %collective-permute-start.13 = (bf16[32,1,128]{2,0,1:T(8,128)(2,1)}, bf16[32,1,128]{2,0,1:T(8,128)(2,1)}, u32[]{:S(2)}, u32[]{:S(2)}) collective-permute-start(bf16[32,1,128]{2,0,1:T(8,128)(2,1)} %slice.401), channel_id=1, source_target_pairs={{2,0},{4,2},{6,4},{8,6},{10,8},{12,10},{14,12},{16,14},{18,16},{20... | collective-permute-start | bytes 24584 | tf_op jit(solution)/shard_map/ppermute | solution.py:13
  477.1 40.4 %collective-permute-start.14 = (bf16[32,1,128]{2,0,1:T(8,128)(2,1)}, bf16[32,1,128]{2,0,1:T(8,128)(2,1)S(1)}, u32[]{:S(2)}, u32[]{:S(2)}) collective-permute-start(bf16[32,1,128]{2,0,1:T(8,128)(2,1)} %get-tuple-element.107), channel_id=1, source_target_pairs={{0,2},{2,4},{4,6},{6,8},{8,10},{10,12},{12,14},{14,16},{16,18},{18... | collective-permute-start | bytes 24584 | tf_op jit(solution)/shard_map/ppermute | solution.py:13
  515.9 5.7 %collective-permute-start.15 = (bf16[32,1,128]{2,0,1:T(8,128)(2,1)S(1)}, bf16[32,1,128]{2,0,1:T(8,128)(2,1)S(1)}, u32[]{:S(2)}, u32[]{:S(2)}) collective-permute-start(bf16[32,1,128]{2,0,1:T(8,128)(2,1)S(1)} %slice.407), channel_id=1, source_target_pairs={{2,0},{4,2},{6,4},{8,6},{10,8},{12,10},{14,12},{16,14},{18,16},{20... | collective-permute-start | bytes 24584 | tf_op jit(solution)/shard_map/ppermute | solution.py:13
  517.5 4.8 copy-start.20
  517.5 4.8 copy-start.62
  (68 other events, 134.8 us)
